TPU v7x, 32 devices: a whole 2x2x4 slice. The times are simulated.
32 devices in a mesh: group: 2 (over y), tile: 4 (over z), strip: 2 (over x), sub: 2 (over core).
Axes of the slice: x: 2, y: 2, z: 4, core: 2. Of those that a mesh axis runs over, the one named last changes fastest.
Arguments:
- right_side: float32 [32, 128, 1024], P('group', 'tile', ('strip', 'sub')), parts along dimension 0, may hold values from -24 to 24
- horiz_coef: float32 [256, 1024], P(('group', 'tile'), ('strip', 'sub')), parts along dimension 0, may hold values from 8 to 32
- vert_coef: float32 [256, 1024], P(('group', 'tile'), ('strip', 'sub')), parts along dimension 0, may hold values from 1 to 8
- panel_owner: int32 [16384, 1], P(('group', 'tile', 'strip', 'sub')), parts along dimension 0, may hold values from 0 to 3; in each aligned block of 512 rows (0 to 511, 512 to 1023, ...) at most 384 rows name the same one
- panel_cell: int32 [16384], P(('group', 'tile', 'strip', 'sub')), parts along dimension 0, may hold values from 0 to 8191
- panel_pressure: float32 [16384], P(('group', 'tile', 'strip', 'sub')), parts along dimension 0, may hold values from -48 to 48
Outputs:
- potential: float32 [32, 128, 1024], P('group', 'tile', ('strip', 'sub')), parts along dimension 0
- residual: float32 [32, 128, 1024], P('group', 'tile', ('strip', 'sub')), parts along dimension 0
There are 2 independent parts, one for each index of `group`. A program takes and returns all parts, laid end to end along the dimension named above; each array names one. Nothing has to cross between parts.
Inputs may be any that keep to these rules, and one draw needn't show every extreme that they name: `panel_owner`: among the 512 panels of one device at most 384 name one owner; some device reaches 384 in every draw.
All inputs are finite; a program needn't handle non-finite values.
Results may differ from a plain program's by a relative error of at most 0.00015.
Values sent between devices are 32-bit elements; how exact they have to be, the bound alone decides.
A program may use at most 128 MiB of HBM per device.

v0:
```python
import functools

import jax
import jax.numpy as jnp
from jax import lax
from jax.experimental import pallas as pl
from jax.experimental.pallas import tpu as pltpu
from jax.sharding import PartitionSpec as P

MESH = pl.DeviceIdType.MESH
OMEGA = 0.8
NZ = 16
ND = 24
SLOT = 16
HALO = (4, 5, 9)
REACH = (1, 1, 2)


def split3(x):
    a = x.astype(jnp.bfloat16)
    y = x - a.astype(jnp.float32)
    b = y.astype(jnp.bfloat16)
    c = (y - b.astype(jnp.float32)).astype(jnp.bfloat16)
    return a, b, c


def dot3(x, m):
    out = None
    for part in split3(x):
        d = jnp.dot(part, m, preferred_element_type=jnp.float32)
        out = d if out is None else out + d
    return out


def down_matrix(rows, cols):
    i = lax.broadcasted_iota(jnp.int32, (rows, cols), 0)
    j = lax.broadcasted_iota(jnp.int32, (rows, cols), 1)
    return jnp.where((i == 2 * j) | (i == 2 * j + 1), 1.0, 0.0).astype(jnp.bfloat16)


def up_matrix(rows, cols, local):
    i = lax.broadcasted_iota(jnp.int32, (rows, cols), 0)
    j = lax.broadcasted_iota(jnp.int32, (rows, cols), 1)
    right = (2 * i == j) | (2 * i + 1 == j)
    ib, jb = 2 * (i - rows), j - cols
    left = (ib == jb) | (ib + 1 == jb)
    hit = ((j < local + 64) & right) | ((j >= local + 64) & left)
    return jnp.where(hit, 1.0, 0.0).astype(jnp.bfloat16)


def kernel(
    dims, rs, kh, kv, owner, cell, pressure, pot, res,
    fpart, frecv, stack, e0, e1, e2, ua0, ub0, rd0, ua1, ub1, rd1, ua2, ub2, rd2,
    t0, t1, rfine, ps0, ps1, ps2, pr0, pr1, pr2, fs_sem, fr_sem, ss, rsem,
):
    tiles, columns, subs = dims
    nx, ny = rs.shape[1], rs.shape[2]
    sizes = (nx, nx // 2, nx // 4)
    widths = (ny, ny // 2, ny // 4)
    es, pss, prs = (e0, e1, e2), (ps0, ps1, ps2), (pr0, pr1, pr2)
    me = lax.axis_index("tile")
    col = lax.axis_index("strip") * subs + lax.axis_index("sub")

    def device(dt, dc):
        c = col + dc
        return {"tile": me + dt, "strip": c // subs, "sub": c % subs}

    def exists(dt, dc):
        ok = jnp.bool_(True)
        if dt:
            t = me + dt
            ok = ok & (t >= 0) & (t < tiles)
        if dc:
            c = col + dc
            ok = ok & (c >= 0) & (c < columns)
        return ok

    for ref in (e0, e1, e2, pr0, pr1, pr2):
        ref[...] = jnp.zeros_like(ref)

    barrier = pltpu.get_barrier_semaphore()
    near = [(dt, dc) for dt in range(-2, 3) for dc in (-1, 0, 1) if dc]
    expected = jnp.int32(tiles - 1)
    for k in range(1, tiles):
        pl.semaphore_signal(barrier, inc=1, device_id={"tile": (me + k) % tiles}, device_id_type=MESH)
    for dt, dc in near:
        ok = exists(dt, dc)
        expected = expected + ok.astype(jnp.int32)

        @pl.when(ok)
        def _():
            pl.semaphore_signal(barrier, inc=1, device_id=device(dt, dc), device_id_type=MESH)

    for ref in (ua0, ub0, ua1, ub1, ua2, ub2):
        ref[...] = jnp.zeros_like(ref)

    g = owner[...] * nx + cell[...] // ny
    y = cell[...] % ny
    parts = split3(pressure[...])
    left, right = [], []
    q = g.shape[0]
    ix = lax.broadcasted_iota(jnp.int32, (tiles * nx, 128), 0)
    iy = lax.broadcasted_iota(jnp.int32, (ny, 128), 0)
    for k in range(q):
        hit = ix == g[k:k + 1]
        left.append(jnp.concatenate(
            [jnp.where(hit, p.astype(jnp.float32)[k:k + 1], 0.0).astype(jnp.bfloat16) for p in parts], 0))
        right.append(jnp.where(iy == y[k:k + 1], 1.0, 0.0).astype(jnp.bfloat16))
    f3 = lax.dot_general(jnp.concatenate(left, 1), jnp.concatenate(right, 1), (((1,), (1,)), ((), ())),
                         preferred_element_type=jnp.float32)
    n = tiles * nx
    fpart[...] = (f3[:n] + f3[n:2 * n] + f3[2 * n:]).reshape(tiles, nx, ny)

    pl.semaphore_wait(barrier, expected)

    copies = []
    for k in range(1, tiles):
        to = (me + k) % tiles
        c = pltpu.make_async_remote_copy(
            src_ref=fpart.at[to], dst_ref=frecv.at[k - 1], send_sem=fs_sem.at[k - 1],
            recv_sem=fr_sem.at[k - 1], device_id={"tile": to}, device_id_type=MESH)
        c.start()
        copies.append(c)
    stack[0:NZ] = rs[...]
    stack[NZ] = kh[...]
    stack[NZ + 1] = kv[...]
    for k in range(NZ + 2, ND):
        stack[k] = jnp.zeros((nx, ny), jnp.float32)
    for c in copies:
        c.wait()
    force = fpart[me]
    for k in range(tiles - 1):
        force = force + frecv[k]
    stack[NZ - 1] = rs[NZ - 1] + force
    h0 = HALO[0]
    e0[h0:h0 + nx, :, 0:ny] = jnp.swapaxes(stack[...], 0, 1)

    lane = lax.broadcasted_iota(jnp.int32, (1, 128), 1)

    def exchange(level):
        e, ps, pr, h, n, w = es[level], pss[level], prs[level], HALO[level], sizes[level], widths[level]
        wt = e.shape[2]
        npk = n // 8
        edge = ((0, 0), ((w - 1) // 128 * 128, (w - SLOT) % 128))
        for side in (0, 1):
            base, off = edge[side]
            for k in range(npk):
                acc = None
                for j in range(8):
                    v = e[h + 8 * k + j, :, base:base + 128]
                    shift = (SLOT * j - off) % 128
                    v = pltpu.roll(v, shift, 1) if shift else v
                    acc = v if acc is None else jnp.where(lane >= SLOT * j, v, acc)
                ps[side, k] = acc
        index = 0
        pending = []
        for dt in range(-REACH[level], REACH[level] + 1):
            for dc in (-1, 0, 1):
                if not (dt or dc):
                    continue
                d = abs(dt)
                if dc == 0:
                    m = min(n, h - (d - 1) * n)
                    send_lo = h if dt < 0 else h + n - m
                    land = h + d * n if dt < 0 else h - (d - 1) * n - m
                    lanes = pl.ds(0, max(w, 128))
                    src = e.at[pl.ds(send_lo, m), :, lanes]
                    dst = e.at[pl.ds(land, m), :, lanes]
                else:
                    side = 0 if dc < 0 else 1
                    slot = (-dt + REACH[level]) * 2 + (1 if dc < 0 else 0)
                    if dt == 0:
                        src, dst = ps.at[side], pr.at[slot]
                    else:
                        k = 0 if dt < 0 else npk - 1
                        src, dst = ps.at[side, pl.ds(k, 1)], pr.at[slot, pl.ds(0, 1)]
                c = pltpu.make_async_remote_copy(
                    src_ref=src, dst_ref=dst, send_sem=ss.at[level, index], recv_sem=rsem.at[level, index],
                    device_id=device(dt, dc), device_id_type=MESH)
                pending.append((c, exists(dt, dc), exists(-dt, -dc)))
                index += 1
        for c, to, _ in pending:
            pl.when(to)(c.start)
        for c, to, _ in pending:
            pl.when(to)(c.wait_send)
        for c, _, come in pending:
            pl.when(come)(c.wait_recv)
        rbase, roff = w // 128 * 128, w % 128
        hb = wt - 128

        def put(row, dt, k, j):
            slot = (dt + REACH[level]) * 2
            from_left = pr[slot, k]
            from_right = pr[slot + 1, k]
            s1 = (128 - SLOT - SLOT * j) % 128
            s2 = (roff - SLOT * j) % 128
            from_left = pltpu.roll(from_left, s1, 1) if s1 else from_left
            from_right = pltpu.roll(from_right, s2, 1) if s2 else from_right
            own = e[row, :, hb:hb + 128] if roff else jnp.zeros((ND, 128), jnp.float32)
            inner = jnp.where((lane >= roff) & (lane < roff + SLOT), from_right, own)
            e[row, :, hb:hb + 128] = jnp.where(lane >= 128 - SLOT, from_left, inner)

        for r in range(n):
            put(h + r, 0, r // 8, r % 8)
        for d in range(1, REACH[level] + 1):
            m = min(n, h - (d - 1) * n)
            for r in range(m):
                put(h - (d - 1) * n - m + r, -d, 0, (n - m + r) % 8)
                put(h + d * n + r, d, 0, r % 8)

    z = lax.broadcasted_iota(jnp.int32, (1, NZ, 1), 1)

    def diag_of(k_h, k_v):
        return 4.0 * k_h + k_v * jnp.where(z > 0, 2.0, 1.0)

    def coefs(e, r, count, scale):
        return scale * e[pl.ds(r, count), NZ:NZ + 1, :], e[pl.ds(r, count), NZ + 1:NZ + 2, :]

    def over(lo, hi, step, fn):
        def loop(i, carry):
            fn(lo + i * step)
            return carry
        lax.fori_loop(0, (hi - lo) // step, loop, 0)

    def first(e, rd, u, scale, rows):
        def at(r):
            k_h, k_v = coefs(e, r, 2, scale)
            diag = diag_of(k_h, k_v)
            inv = jnp.where(diag > 0.0, OMEGA / diag, 0.0)
            rd[pl.ds(r, 2)] = inv
            u[pl.ds(r + 1, 2)] = inv * e[pl.ds(r, 2), 0:NZ, :]
        over(0, rows, 2, at)

    def terms(e, u, r, count, scale):
        wt = u.shape[2]
        k_h, k_v = coefs(e, r, count, scale)
        x = u[pl.ds(r + 1, count)]
        hs = u[pl.ds(r, count)] + u[pl.ds(r + 2, count)]
        hs = hs + pltpu.roll(x, 1, 2) + pltpu.roll(x, wt - 1, 2)
        vs = jnp.where(z < NZ - 1, pltpu.roll(x, NZ - 1, 1), 0.0) + jnp.where(z > 0, pltpu.roll(x, 1, 1), 0.0)
        return x, e[pl.ds(r, count), 0:NZ, :] + k_h * hs + k_v * vs, k_h, k_v

    def sweep(e, rd, u, v, scale, rows):
        def at(r):
            x, t, _, _ = terms(e, u, r, 2, scale)
            v[pl.ds(r + 1, 2)] = (1.0 - OMEGA) * x + rd[pl.ds(r, 2)] * t
        over(0, rows, 2, at)

    def residue(e, u, r, count, scale):
        x, t, k_h, k_v = terms(e, u, r, count, scale)
        return t - diag_of(k_h, k_v) * x

    def restrict(level, u, t):
        e, h, n, w = es[level], HALO[level], sizes[level], widths[level]
        scale = 0.25 ** level
        wt = t.shape[2]

        def at(k):
            r = h + 2 * k
            both = residue(e, u, r, 2, scale)[:, :, 0:wt]
            t[k, 0:NZ] = 0.25 * (both[0] + both[1])
            t[k, NZ:ND] = 0.25 * (e[r, NZ:ND, 0:wt] + e[r + 1, NZ:ND, 0:wt])
        over(0, n // 2, 1, at)
        out = dot3(t[...].reshape(n // 2 * ND, wt), down_matrix(wt, 128))
        if w // 2 < 128:
            out = jnp.where(lane < w // 2, out, 0.0)
        es[level + 1][pl.ds(HALO[level + 1], n // 2), :, 0:128] = out.reshape(n // 2, ND, 128)

    def prolong(level, u, lo, count, fine, fine_lo):
        wt, wf = u.shape[2], fine.shape[2]
        m = up_matrix(wt, wf, widths[level - 1])
        rows = dot3(u[lo + 1:lo + 1 + count].reshape(count * NZ, wt), m).reshape(count, NZ, wf)
        for k in range(count):
            for j in range(2):
                f = fine_lo + 1 + 2 * k + j
                fine[f] = fine[f] + rows[k]

    n0, n1, n2 = (sizes[k] + 2 * HALO[k] for k in range(3))
    exchange(0)
    first(e0, rd0, ua0, 1.0, n0)
    sweep(e0, rd0, ua0, ub0, 1.0, n0)
    restrict(0, ub0, t0)
    exchange(1)
    first(e1, rd1, ua1, 0.25, n1)
    sweep(e1, rd1, ua1, ub1, 0.25, n1)
    restrict(1, ub1, t1)
    exchange(2)
    first(e2, rd2, ua2, 0.0625, n2)
    for _ in range(3):
        sweep(e2, rd2, ua2, ub2, 0.0625, n2)
        sweep(e2, rd2, ub2, ua2, 0.0625, n2)
    sweep(e2, rd2, ua2, ub2, 0.0625, n2)
    prolong(2, ub2, HALO[2] - 2, sizes[2] + 4, ub1, HALO[1] - 4)
    sweep(e1, rd1, ub1, ua1, 0.25, n1)
    sweep(e1, rd1, ua1, ub1, 0.25, n1)
    prolong(1, ub1, HALO[1] - 2, sizes[1] + 4, ub0, 0)
    sweep(e0, rd0, ub0, ua0, 1.0, n0)
    sweep(e0, rd0, ua0, ub0, 1.0, n0)

    def last(k):
        rfine[pl.ds(k, 2)] = residue(e0, ub0, h0 + k, 2, 1.0)[:, :, 0:ny]
    over(0, nx, 2, last)
    pot[...] = jnp.swapaxes(ub0[h0 + 1:h0 + 1 + nx, :, 0:ny], 0, 1)
    res[...] = jnp.swapaxes(rfine[...], 0, 1)


def solution(mesh):
    tiles, strips, subs = mesh.shape["tile"], mesh.shape["strip"], mesh.shape["sub"]

    def body(right_side, horiz_coef, vert_coef, panel_owner, panel_cell, panel_pressure):
        nz, nx, ny = right_side.shape
        rows = [n + 2 * h for n, h in zip((nx, nx // 2, nx // 4), HALO)]
        wts = (ny + 128, ny // 2 + 128, 128)
        f32 = jnp.float32
        scratch = [
            pltpu.VMEM((tiles, nx, ny), f32),
            pltpu.VMEM((max(tiles - 1, 1), nx, ny), f32),
            pltpu.VMEM((ND, nx, ny), f32),
        ]
        scratch += [pltpu.VMEM((rows[k], ND, wts[k]), f32) for k in range(3)]
        for k in range(3):
            scratch += [pltpu.VMEM((rows[k] + 2, NZ, wts[k]), f32)] * 2 + [pltpu.VMEM((rows[k], NZ, wts[k]), f32)]
        scratch += [pltpu.VMEM((nx // 2, ND, ny), f32), pltpu.VMEM((nx // 4, ND, ny // 2), f32)]
        scratch += [pltpu.VMEM((nx, NZ, ny), f32)]
        scratch += [pltpu.VMEM((2, nx // 8 >> k, ND, 128), f32) for k in range(3)]
        scratch += [pltpu.VMEM((2 * (2 * REACH[k] + 1), nx // 8 >> k, ND, 128), f32) for k in range(3)]
        scratch += [
            pltpu.SemaphoreType.DMA((max(tiles - 1, 1),)),
            pltpu.SemaphoreType.DMA((max(tiles - 1, 1),)),
            pltpu.SemaphoreType.DMA((3, 14)),
            pltpu.SemaphoreType.DMA((3, 14)),
        ]
        panels = panel_cell.shape[0]
        out = jax.ShapeDtypeStruct((nz, nx, ny), f32)
        vmem = pl.BlockSpec(memory_space=pltpu.VMEM)
        return pl.pallas_call(
            functools.partial(kernel, (tiles, strips * subs, subs)),
            out_shape=(out, out),
            in_specs=[vmem] * 6,
            out_specs=(vmem, vmem),
            scratch_shapes=scratch,
            compiler_params=pltpu.CompilerParams(
                collective_id=0, has_side_effects=True, vmem_limit_bytes=40 * 1024 * 1024
            ),
        )(
            right_side, horiz_coef, vert_coef,
            panel_owner.reshape(panels // 128, 128), panel_cell.reshape(panels // 128, 128),
            panel_pressure.reshape(panels // 128, 128),
        )

    return jax.shard_map(
        body,
        mesh=mesh,
        in_specs=(
            P("group", "tile", ("strip", "sub")),
            P(("group", "tile"), ("strip", "sub")),
            P(("group", "tile"), ("strip", "sub")),
            P(("group", "tile", "strip", "sub"), None),
            P(("group", "tile", "strip", "sub")),
            P(("group", "tile", "strip", "sub")),
        ),
        out_specs=(P("group", "tile", ("strip", "sub")), P("group", "tile", ("strip", "sub"))),
        check_vma=False,
    )
```

profile of v0, /device:TPU:0, one launch (start us, length us, event | category | flops | bytes accessed | tf_op | source)
XLA Modules:
  0.0 55.5 jit_solution(10585873628521791655)
XLA Ops:
  0.6 0.0 copy-start.4
  0.6 0.0 copy-start.3
  0.7 0.7 %copy-done.4 = s32[512]{0:T(512)S(1)} copy-done((s32[512]{0:T(512)S(1)}, s32[512]{0:T(512)}, u32[]{:S(2)}) %copy-start.4) | copy-done | bytes 2072
  1.3 0.0 copy-done.3
  1.3 0.0 copy-start
  1.3 1.0 %copy-done = f32[16,32,256]{2,1,0:T(8,128)S(1)} copy-done((f32[16,32,256]{2,1,0:T(8,128)S(1)}, f32[16,32,256]{2,1,0:T(8,128)}, u32[]{:S(2)}) %copy-start) | copy-done | bytes 524312
  2.4 0.0 copy-start.1
  2.4 0.8 %copy-done.1 = f32[32,256]{1,0:T(8,128)S(1)} copy-done((f32[32,256]{1,0:T(8,128)S(1)}, f32[32,256]{1,0:T(8,128)}, u32[]{:S(2)}) %copy-start.1) | copy-done | bytes 32792
  3.1 0.0 copy-start.2
  3.1 0.8 %copy-done.2 = f32[32,256]{1,0:T(8,128)S(1)} copy-done((f32[32,256]{1,0:T(8,128)S(1)}, f32[32,256]{1,0:T(8,128)}, u32[]{:S(2)}) %copy-start.2) | copy-done | bytes 32792
  3.9 0.0 copy-start.5
  3.9 0.7 %copy-done.5 = f32[512]{0:T(512)S(1)} copy-done((f32[512]{0:T(512)S(1)}, f32[512]{0:T(512)}, u32[]{:S(2)}) %copy-start.5) | copy-done | bytes 2072
  4.6 49.3 %shard_map.77 = (f32[16,32,256]{2,1,0:T(8,128)S(1)}, f32[16,32,256]{2,1,0:T(8,128)S(1)}) custom-call(f32[16,32,256]{2,1,0:T(8,128)S(1)} %copy-done, f32[32,256]{1,0:T(8,128)S(1)} %copy-done.1, f32[32,256]{1,0:T(8,128)S(1)} %copy-done.2, s32[4,128]{1,0:T(4,128)S(1)} %bitcast.3, s32[4,128]{1,0:T(4,128)S(1)} %bitcast.4, f32[4,128]{1,0:T(4,128)S(1)} %bitcast.5), custom_call_target="tpu_custom_call" | custom-call | tf_op jit(solution)/shard_map/pallas_call | solution.py:336
  53.9 0.8 %copy.10 = f32[16,32,256]{2,1,0:T(8,128)} copy(f32[16,32,256]{2,1,0:T(8,128)S(1)} %get-tuple-element.4) | data formatting | bytes 1048576
  54.7 0.8 %copy.11 = f32[16,32,256]{2,1,0:T(8,128)} copy(f32[16,32,256]{2,1,0:T(8,128)S(1)} %get-tuple-element.5) | data formatting | bytes 1048576
Async XLA Ops:
  0.6 0.7 %copy-start.4 = (s32[512]{0:T(512)S(1)}, s32[512]{0:T(512)}, u32[]{:S(2)}) copy-start(s32[512]{0:T(512)} %param.10) | copy-start | bytes 6148
  0.6 0.7 %copy-start.3 = (s32[512,1]{0,1:T(1,128)S(1)}, s32[512,1]{0,1:T(1,128)}, u32[]{:S(2)}) copy-start(s32[512,1]{0,1:T(1,128)} %param.9) | copy-start | bytes 6148
  1.3 1.0 %copy-start = (f32[16,32,256]{2,1,0:T(8,128)S(1)}, f32[16,32,256]{2,1,0:T(8,128)}, u32[]{:S(2)}) copy-start(f32[16,32,256]{2,1,0:T(8,128)} %rs.1) | copy-start | bytes 1572868
  2.4 0.8 %copy-start.1 = (f32[32,256]{1,0:T(8,128)S(1)}, f32[32,256]{1,0:T(8,128)}, u32[]{:S(2)}) copy-start(f32[32,256]{1,0:T(8,128)} %kh.1) | copy-start | bytes 98308
  3.1 0.8 %copy-start.2 = (f32[32,256]{1,0:T(8,128)S(1)}, f32[32,256]{1,0:T(8,128)}, u32[]{:S(2)}) copy-start(f32[32,256]{1,0:T(8,128)} %kv.1) | copy-start | bytes 98308
  3.9 0.7 %copy-start.5 = (f32[512]{0:T(512)S(1)}, f32[512]{0:T(512)}, u32[]{:S(2)}) copy-start(f32[512]{0:T(512)} %param.11) | copy-start | bytes 6148
where the time goes:
time: 55.8 us; the launch traced here: 55.5 us
  Pallas kernels  49.3 us (88%)
  local copies, waits for them, and re-layouts  5.51 us (10%)
  between operations  0.66 us (1%)
    pallas_call x1, Pallas kernels, body(): pl.pallas_call(functools.partial(kernel, (tiles, strips * subs, subs)), o...  49.3 us
    unnamed x14, local copies, waits for them, and re-layouts  5.51 us

commit v1 on v0

--- a/solution.py
+++ b/solution.py
@@ -14,6 +14,7 @@
 SLOT = 16
 HALO = (4, 5, 9)
 REACH = (1, 1, 2)
+BLOCK = (8, 12, 26)
 
 
 def split3(x):
@@ -49,9 +50,10 @@
 
 
 def kernel(
-    dims, rs, kh, kv, owner, cell, pressure, pot, res,
+    dims, rs, kh, kv, owner_in, cell_in, pressure_in, pot, res,
     fpart, frecv, stack, e0, e1, e2, ua0, ub0, rd0, ua1, ub1, rd1, ua2, ub2, rd2,
-    t0, t1, rfine, ps0, ps1, ps2, pr0, pr1, pr2, fs_sem, fr_sem, ss, rsem,
+    t0, t1, rfine, ps0, ps1, ps2, pr0, pr1, pr2, owner, cell, pressure,
+    fs_sem, fr_sem, ss, rsem, in_sem,
 ):
     tiles, columns, subs = dims
     nx, ny = rs.shape[1], rs.shape[2]
@@ -75,8 +77,20 @@
             ok = ok & (c >= 0) & (c < columns)
         return ok
 
-    for ref in (e0, e1, e2, pr0, pr1, pr2):
-        ref[...] = jnp.zeros_like(ref)
+    loads = [
+        pltpu.make_async_copy(src, dst, in_sem.at[k])
+        for k, (src, dst) in enumerate((
+            (owner_in, owner), (cell_in, cell), (pressure_in, pressure),
+            (rs, stack.at[pl.ds(0, NZ)]), (kh, stack.at[NZ]), (kv, stack.at[NZ + 1])))
+    ]
+    for c in loads:
+        c.start()
+    for level in range(3):
+        e, h, n = es[level], HALO[level], sizes[level]
+        wt = e.shape[2]
+        e[0:h] = jnp.zeros((h, ND, wt), jnp.float32)
+        e[h + n:] = jnp.zeros((h, ND, wt), jnp.float32)
+        prs[level][...] = jnp.zeros_like(prs[level])
 
     barrier = pltpu.get_barrier_semaphore()
     near = [(dt, dc) for dt in range(-2, 3) for dc in (-1, 0, 1) if dc]
@@ -92,7 +106,10 @@
             pl.semaphore_signal(barrier, inc=1, device_id=device(dt, dc), device_id_type=MESH)
 
     for ref in (ua0, ub0, ua1, ub1, ua2, ub2):
-        ref[...] = jnp.zeros_like(ref)
+        ref[0] = jnp.zeros(ref.shape[1:], jnp.float32)
+        ref[ref.shape[0] - 1] = jnp.zeros(ref.shape[1:], jnp.float32)
+    for c in loads[:3]:
+        c.wait()
 
     g = owner[...] * nx + cell[...] // ny
     y = cell[...] % ny
@@ -121,19 +138,21 @@
             recv_sem=fr_sem.at[k - 1], device_id={"tile": to}, device_id_type=MESH)
         c.start()
         copies.append(c)
-    stack[0:NZ] = rs[...]
-    stack[NZ] = kh[...]
-    stack[NZ + 1] = kv[...]
     for k in range(NZ + 2, ND):
         stack[k] = jnp.zeros((nx, ny), jnp.float32)
+    for c in loads[3:]:
+        c.wait()
+    h0 = HALO[0]
+    e0[h0:h0 + nx, :, 0:ny] = jnp.swapaxes(stack[...], 0, 1)
     for c in copies:
         c.wait()
     force = fpart[me]
     for k in range(tiles - 1):
         force = force + frecv[k]
-    stack[NZ - 1] = rs[NZ - 1] + force
-    h0 = HALO[0]
-    e0[h0:h0 + nx, :, 0:ny] = jnp.swapaxes(stack[...], 0, 1)
+    stack[NZ + 2] = force
+    top = lax.broadcasted_iota(jnp.int32, (8, 1), 0) == 7
+    for r in range(nx):
+        e0[h0 + r, NZ - 8:NZ, 0:ny] += jnp.where(top, stack[NZ + 2, r:r + 1, :], 0.0)
 
     lane = lax.broadcasted_iota(jnp.int32, (1, 128), 1)
 
@@ -185,7 +204,7 @@
             pl.when(to)(c.wait_send)
         for c, _, come in pending:
             pl.when(come)(c.wait_recv)
-        rbase, roff = w // 128 * 128, w % 128
+        roff = w % 128
         hb = wt - 128
 
         def put(row, dt, k, j):
@@ -216,20 +235,32 @@
     def coefs(e, r, count, scale):
         return scale * e[pl.ds(r, count), NZ:NZ + 1, :], e[pl.ds(r, count), NZ + 1:NZ + 2, :]
 
-    def over(lo, hi, step, fn):
+    def over(lo, hi, step, fn, block):
+        if hi - lo <= block:
+            for r in range(lo, hi, step):
+                fn(r)
+            return
+
         def loop(i, carry):
-            fn(lo + i * step)
+            for j in range(0, block, step):
+                fn(lo + i * block + j)
             return carry
-        lax.fori_loop(0, (hi - lo) // step, loop, 0)
+        lax.fori_loop(0, (hi - lo) // block, loop, 0)
+        for r in range(lo + (hi - lo) // block * block, hi, step):
+            fn(r)
+
+    def block_of(e):
+        return BLOCK[[x is e for x in es].index(True)]
 
     def first(e, rd, u, scale, rows):
         def at(r):
             k_h, k_v = coefs(e, r, 2, scale)
-            diag = diag_of(k_h, k_v)
+            diag = 4.0 * k_h + k_v * jnp.where(z[:, 0:8] > 0, 2.0, 1.0)
             inv = jnp.where(diag > 0.0, OMEGA / diag, 0.0)
             rd[pl.ds(r, 2)] = inv
-            u[pl.ds(r + 1, 2)] = inv * e[pl.ds(r, 2), 0:NZ, :]
-        over(0, rows, 2, at)
+            u[pl.ds(r + 1, 2), 0:8] = inv * e[pl.ds(r, 2), 0:8, :]
+            u[pl.ds(r + 1, 2), 8:16] = inv[:, 1:2] * e[pl.ds(r, 2), 8:16, :]
+        over(0, rows, 2, at, block_of(e))
 
     def terms(e, u, r, count, scale):
         wt = u.shape[2]
@@ -240,11 +271,13 @@
         vs = jnp.where(z < NZ - 1, pltpu.roll(x, NZ - 1, 1), 0.0) + jnp.where(z > 0, pltpu.roll(x, 1, 1), 0.0)
         return x, e[pl.ds(r, count), 0:NZ, :] + k_h * hs + k_v * vs, k_h, k_v
 
-    def sweep(e, rd, u, v, scale, rows):
+    def sweep(e, rd, u, v, scale, rows, cut=0):
         def at(r):
             x, t, _, _ = terms(e, u, r, 2, scale)
-            v[pl.ds(r + 1, 2)] = (1.0 - OMEGA) * x + rd[pl.ds(r, 2)] * t
-        over(0, rows, 2, at)
+            x = (1.0 - OMEGA) * x
+            v[pl.ds(r + 1, 2), 0:8] = x[:, 0:8] + rd[pl.ds(r, 2)] * t[:, 0:8]
+            v[pl.ds(r + 1, 2), 8:16] = x[:, 8:16] + rd[pl.ds(r, 2), 1:2] * t[:, 8:16]
+        over(cut, rows - cut, 2, at, block_of(e))
 
     def residue(e, u, r, count, scale):
         x, t, k_h, k_v = terms(e, u, r, count, scale)
@@ -260,7 +293,7 @@
             both = residue(e, u, r, 2, scale)[:, :, 0:wt]
             t[k, 0:NZ] = 0.25 * (both[0] + both[1])
             t[k, NZ:ND] = 0.25 * (e[r, NZ:ND, 0:wt] + e[r + 1, NZ:ND, 0:wt])
-        over(0, n // 2, 1, at)
+        over(0, n // 2, 1, at, 4)
         out = dot3(t[...].reshape(n // 2 * ND, wt), down_matrix(wt, 128))
         if w // 2 < 128:
             out = jnp.where(lane < w // 2, out, 0.0)
@@ -278,28 +311,28 @@
     n0, n1, n2 = (sizes[k] + 2 * HALO[k] for k in range(3))
     exchange(0)
     first(e0, rd0, ua0, 1.0, n0)
-    sweep(e0, rd0, ua0, ub0, 1.0, n0)
+    sweep(e0, rd0, ua0, ub0, 1.0, n0, 1)
     restrict(0, ub0, t0)
     exchange(1)
     first(e1, rd1, ua1, 0.25, n1)
-    sweep(e1, rd1, ua1, ub1, 0.25, n1)
+    sweep(e1, rd1, ua1, ub1, 0.25, n1, 1)
     restrict(1, ub1, t1)
     exchange(2)
     first(e2, rd2, ua2, 0.0625, n2)
-    for _ in range(3):
-        sweep(e2, rd2, ua2, ub2, 0.0625, n2)
-        sweep(e2, rd2, ub2, ua2, 0.0625, n2)
-    sweep(e2, rd2, ua2, ub2, 0.0625, n2)
+    for k in range(3):
+        sweep(e2, rd2, ua2, ub2, 0.0625, n2, 2 * k + 1)
+        sweep(e2, rd2, ub2, ua2, 0.0625, n2, 2 * k + 2)
+    sweep(e2, rd2, ua2, ub2, 0.0625, n2, 7)
     prolong(2, ub2, HALO[2] - 2, sizes[2] + 4, ub1, HALO[1] - 4)
-    sweep(e1, rd1, ub1, ua1, 0.25, n1)
-    sweep(e1, rd1, ua1, ub1, 0.25, n1)
+    sweep(e1, rd1, ub1, ua1, 0.25, n1, 2)
+    sweep(e1, rd1, ua1, ub1, 0.25, n1, 3)
     prolong(1, ub1, HALO[1] - 2, sizes[1] + 4, ub0, 0)
-    sweep(e0, rd0, ub0, ua0, 1.0, n0)
-    sweep(e0, rd0, ua0, ub0, 1.0, n0)
+    sweep(e0, rd0, ub0, ua0, 1.0, n0, 2)
+    sweep(e0, rd0, ua0, ub0, 1.0, n0, 3)
 
     def last(k):
         rfine[pl.ds(k, 2)] = residue(e0, ub0, h0 + k, 2, 1.0)[:, :, 0:ny]
-    over(0, nx, 2, last)
+    over(0, nx, 2, last, 8)
     pot[...] = jnp.swapaxes(ub0[h0 + 1:h0 + 1 + nx, :, 0:ny], 0, 1)
     res[...] = jnp.swapaxes(rfine[...], 0, 1)
 
@@ -319,24 +352,26 @@
         ]
         scratch += [pltpu.VMEM((rows[k], ND, wts[k]), f32) for k in range(3)]
         for k in range(3):
-            scratch += [pltpu.VMEM((rows[k] + 2, NZ, wts[k]), f32)] * 2 + [pltpu.VMEM((rows[k], NZ, wts[k]), f32)]
+            scratch += [pltpu.VMEM((rows[k] + 2, NZ, wts[k]), f32)] * 2 + [pltpu.VMEM((rows[k], 8, wts[k]), f32)]
         scratch += [pltpu.VMEM((nx // 2, ND, ny), f32), pltpu.VMEM((nx // 4, ND, ny // 2), f32)]
         scratch += [pltpu.VMEM((nx, NZ, ny), f32)]
         scratch += [pltpu.VMEM((2, nx // 8 >> k, ND, 128), f32) for k in range(3)]
         scratch += [pltpu.VMEM((2 * (2 * REACH[k] + 1), nx // 8 >> k, ND, 128), f32) for k in range(3)]
+        panels = panel_cell.shape[0]
+        scratch += [pltpu.VMEM((panels // 128, 128), t) for t in (jnp.int32, jnp.int32, f32)]
         scratch += [
             pltpu.SemaphoreType.DMA((max(tiles - 1, 1),)),
             pltpu.SemaphoreType.DMA((max(tiles - 1, 1),)),
             pltpu.SemaphoreType.DMA((3, 14)),
             pltpu.SemaphoreType.DMA((3, 14)),
+            pltpu.SemaphoreType.DMA((6,)),
         ]
-        panels = panel_cell.shape[0]
         out = jax.ShapeDtypeStruct((nz, nx, ny), f32)
         vmem = pl.BlockSpec(memory_space=pltpu.VMEM)
         return pl.pallas_call(
             functools.partial(kernel, (tiles, strips * subs, subs)),
             out_shape=(out, out),
-            in_specs=[vmem] * 6,
+            in_specs=[pl.BlockSpec(memory_space=pltpu.HBM)] * 6,
             out_specs=(vmem, vmem),
             scratch_shapes=scratch,
             compiler_params=pltpu.CompilerParams(

time: 55.8 us -> 39.9 us (0.72)
  Pallas kernels: 49.3 us -> 33.4 us
    pallas_call x1, Pallas kernels: 49.3 us -> 33.4 us  [body(): pl.pallas_call(functools.partial(kernel, (tiles, strips * subs, subs)), o...]
where the time goes in v1:
time: 39.9 us; the launch traced here: 39.6 us
  Pallas kernels  33.4 us (84%)
  local copies, waits for them, and re-layouts  5.51 us (14%)
  between operations  0.66 us (2%)
    pallas_call x1, Pallas kernels, body(): pl.pallas_call(functools.partial(kernel, (tiles, strips * subs, subs)), o...  33.4 us
    unnamed x14, local copies, waits for them, and re-layouts  5.51 us

profile of v1, /device:TPU:0, one launch (start us, length us, event | category | flops | bytes accessed | tf_op | source)
XLA Modules:
  0.0 39.6 jit_solution(2052204988652480278)
XLA Ops:
  0.6 0.0 copy-start.4
  0.6 0.0 copy-start.3
  0.7 0.7 %copy-done.4 = s32[512]{0:T(512)S(1)} copy-done((s32[512]{0:T(512)S(1)}, s32[512]{0:T(512)}, u32[]{:S(2)}) %copy-start.4) | copy-done | bytes 2072
  1.3 0.0 copy-done.3
  1.3 0.0 copy-start
  1.3 1.0 %copy-done = f32[16,32,256]{2,1,0:T(8,128)S(1)} copy-done((f32[16,32,256]{2,1,0:T(8,128)S(1)}, f32[16,32,256]{2,1,0:T(8,128)}, u32[]{:S(2)}) %copy-start) | copy-done | bytes 524312
  2.4 0.0 copy-start.1
  2.4 0.8 %copy-done.1 = f32[32,256]{1,0:T(8,128)S(1)} copy-done((f32[32,256]{1,0:T(8,128)S(1)}, f32[32,256]{1,0:T(8,128)}, u32[]{:S(2)}) %copy-start.1) | copy-done | bytes 32792
  3.1 0.0 copy-start.2
  3.1 0.8 %copy-done.2 = f32[32,256]{1,0:T(8,128)S(1)} copy-done((f32[32,256]{1,0:T(8,128)S(1)}, f32[32,256]{1,0:T(8,128)}, u32[]{:S(2)}) %copy-start.2) | copy-done | bytes 32792
  3.9 0.0 copy-start.5
  3.9 0.7 %copy-done.5 = f32[512]{0:T(512)S(1)} copy-done((f32[512]{0:T(512)S(1)}, f32[512]{0:T(512)}, u32[]{:S(2)}) %copy-start.5) | copy-done | bytes 2072
  4.6 33.4 %shard_map.77 = (f32[16,32,256]{2,1,0:T(8,128)S(1)}, f32[16,32,256]{2,1,0:T(8,128)S(1)}) custom-call(f32[16,32,256]{2,1,0:T(8,128)S(1)} %copy-done, f32[32,256]{1,0:T(8,128)S(1)} %copy-done.1, f32[32,256]{1,0:T(8,128)S(1)} %copy-done.2, s32[4,128]{1,0:T(4,128)S(1)} %bitcast.3, s32[4,128]{1,0:T(4,128)S(1)} %bitcast.4, f32[4,128]{1,0:T(4,128)S(1)} %bitcast.5), custom_call_target="tpu_custom_call" | custom-call | tf_op jit(solution)/shard_map/pallas_call | solution.py:371
  38.0 0.8 %copy.10 = f32[16,32,256]{2,1,0:T(8,128)} copy(f32[16,32,256]{2,1,0:T(8,128)S(1)} %get-tuple-element.4) | data formatting | bytes 1048576
  38.8 0.8 %copy.11 = f32[16,32,256]{2,1,0:T(8,128)} copy(f32[16,32,256]{2,1,0:T(8,128)S(1)} %get-tuple-element.5) | data formatting | bytes 1048576
Async XLA Ops:
  0.6 0.7 %copy-start.4 = (s32[512]{0:T(512)S(1)}, s32[512]{0:T(512)}, u32[]{:S(2)}) copy-start(s32[512]{0:T(512)} %param.10) | copy-start | bytes 6148
  0.6 0.7 %copy-start.3 = (s32[512,1]{0,1:T(1,128)S(1)}, s32[512,1]{0,1:T(1,128)}, u32[]{:S(2)}) copy-start(s32[512,1]{0,1:T(1,128)} %param.9) | copy-start | bytes 6148
  1.3 1.0 %copy-start = (f32[16,32,256]{2,1,0:T(8,128)S(1)}, f32[16,32,256]{2,1,0:T(8,128)}, u32[]{:S(2)}) copy-start(f32[16,32,256]{2,1,0:T(8,128)} %rs.1) | copy-start | bytes 1572868
  2.4 0.8 %copy-start.1 = (f32[32,256]{1,0:T(8,128)S(1)}, f32[32,256]{1,0:T(8,128)}, u32[]{:S(2)}) copy-start(f32[32,256]{1,0:T(8,128)} %kh.1) | copy-start | bytes 98308
  3.1 0.8 %copy-start.2 = (f32[32,256]{1,0:T(8,128)S(1)}, f32[32,256]{1,0:T(8,128)}, u32[]{:S(2)}) copy-start(f32[32,256]{1,0:T(8,128)} %kv.1) | copy-start | bytes 98308
  3.9 0.7 %copy-start.5 = (f32[512]{0:T(512)S(1)}, f32[512]{0:T(512)}, u32[]{:S(2)}) copy-start(f32[512]{0:T(512)} %param.11) | copy-start | bytes 6148

commit v2 on v1

--- a/solution.py
+++ b/solution.py
@@ -9,6 +9,7 @@
 
 MESH = pl.DeviceIdType.MESH
 OMEGA = 0.8
+VMEM_BYTES = 64 * 1024 * 1024
 NZ = 16
 ND = 24
 SLOT = 16
@@ -25,12 +26,12 @@
     return a, b, c
 
 
-def dot3(x, m):
-    out = None
-    for part in split3(x):
-        d = jnp.dot(part, m, preferred_element_type=jnp.float32)
-        out = d if out is None else out + d
-    return out
+def dot2(x, m):
+    a = x.astype(jnp.bfloat16)
+    b = (x - a.astype(jnp.float32)).astype(jnp.bfloat16)
+    n = x.shape[0]
+    out = jnp.dot(jnp.concatenate([a, b], 0), m, preferred_element_type=jnp.float32)
+    return out[:n] + out[n:]
 
 
 def down_matrix(rows, cols):
@@ -52,7 +53,7 @@
 def kernel(
     dims, rs, kh, kv, owner_in, cell_in, pressure_in, pot, res,
     fpart, frecv, stack, e0, e1, e2, ua0, ub0, rd0, ua1, ub1, rd1, ua2, ub2, rd2,
-    t0, t1, rfine, ps0, ps1, ps2, pr0, pr1, pr2, owner, cell, pressure,
+    t0, t1, rfine, ps0, ps1, ps2, pr0, pr1, pr2, owner, cell, pressure, out_pot, out_res, rows_out, rows_in,
     fs_sem, fr_sem, ss, rsem, in_sem,
 ):
     tiles, columns, subs = dims
@@ -91,6 +92,7 @@
         e[0:h] = jnp.zeros((h, ND, wt), jnp.float32)
         e[h + n:] = jnp.zeros((h, ND, wt), jnp.float32)
         prs[level][...] = jnp.zeros_like(prs[level])
+    rows_in[...] = jnp.zeros_like(rows_in)
 
     barrier = pltpu.get_barrier_semaphore()
     near = [(dt, dc) for dt in range(-2, 3) for dc in (-1, 0, 1) if dc]
@@ -171,6 +173,9 @@
                     v = pltpu.roll(v, shift, 1) if shift else v
                     acc = v if acc is None else jnp.where(lane >= SLOT * j, v, acc)
                 ps[side, k] = acc
+        if level == 2:
+            for k in range(n // 2):
+                rows_out[k] = e[h + k] + pltpu.roll(e[h + k + n // 2], 64, 1)
         index = 0
         pending = []
         for dt in range(-REACH[level], REACH[level] + 1):
@@ -185,6 +190,8 @@
                     lanes = pl.ds(0, max(w, 128))
                     src = e.at[pl.ds(send_lo, m), :, lanes]
                     dst = e.at[pl.ds(land, m), :, lanes]
+                    if level == 2 and d == 1:
+                        src, dst = rows_out, rows_in.at[(1 - dt) // 2]
                 else:
                     side = 0 if dc < 0 else 1
                     slot = (-dt + REACH[level]) * 2 + (1 if dc < 0 else 0)
@@ -204,6 +211,13 @@
             pl.when(to)(c.wait_send)
         for c, _, come in pending:
             pl.when(come)(c.wait_recv)
+        if level == 2:
+            for k in range(n // 2):
+                for side in (0, 1):
+                    row = k + h + (2 * side - 1) * n
+                    both = rows_in[side, k]
+                    e[row] = jnp.where(lane < w, both, 0.0)
+                    e[row + n // 2] = jnp.where(lane < w, pltpu.roll(both, 64, 1), 0.0)
         roff = w % 128
         hb = wt - 128
 
@@ -294,7 +308,7 @@
             t[k, 0:NZ] = 0.25 * (both[0] + both[1])
             t[k, NZ:ND] = 0.25 * (e[r, NZ:ND, 0:wt] + e[r + 1, NZ:ND, 0:wt])
         over(0, n // 2, 1, at, 4)
-        out = dot3(t[...].reshape(n // 2 * ND, wt), down_matrix(wt, 128))
+        out = dot2(t[...].reshape(n // 2 * ND, wt), down_matrix(wt, 128))
         if w // 2 < 128:
             out = jnp.where(lane < w // 2, out, 0.0)
         es[level + 1][pl.ds(HALO[level + 1], n // 2), :, 0:128] = out.reshape(n // 2, ND, 128)
@@ -302,7 +316,7 @@
     def prolong(level, u, lo, count, fine, fine_lo):
         wt, wf = u.shape[2], fine.shape[2]
         m = up_matrix(wt, wf, widths[level - 1])
-        rows = dot3(u[lo + 1:lo + 1 + count].reshape(count * NZ, wt), m).reshape(count, NZ, wf)
+        rows = dot2(u[lo + 1:lo + 1 + count].reshape(count * NZ, wt), m).reshape(count, NZ, wf)
         for k in range(count):
             for j in range(2):
                 f = fine_lo + 1 + 2 * k + j
@@ -330,11 +344,18 @@
     sweep(e0, rd0, ub0, ua0, 1.0, n0, 2)
     sweep(e0, rd0, ua0, ub0, 1.0, n0, 3)
 
+    out_pot[...] = jnp.swapaxes(ub0[h0 + 1:h0 + 1 + nx, :, 0:ny], 0, 1)
+    store = pltpu.make_async_copy(out_pot, pot, in_sem.at[6])
+    store.start()
+
     def last(k):
         rfine[pl.ds(k, 2)] = residue(e0, ub0, h0 + k, 2, 1.0)[:, :, 0:ny]
     over(0, nx, 2, last, 8)
-    pot[...] = jnp.swapaxes(ub0[h0 + 1:h0 + 1 + nx, :, 0:ny], 0, 1)
-    res[...] = jnp.swapaxes(rfine[...], 0, 1)
+    out_res[...] = jnp.swapaxes(rfine[...], 0, 1)
+    final = pltpu.make_async_copy(out_res, res, in_sem.at[7])
+    final.start()
+    store.wait()
+    final.wait()
 
 
 def solution(mesh):
@@ -359,23 +380,26 @@
         scratch += [pltpu.VMEM((2 * (2 * REACH[k] + 1), nx // 8 >> k, ND, 128), f32) for k in range(3)]
         panels = panel_cell.shape[0]
         scratch += [pltpu.VMEM((panels // 128, 128), t) for t in (jnp.int32, jnp.int32, f32)]
+        scratch += [pltpu.VMEM((nz, nx, ny), f32)] * 2
+        half = nx // 8
+        scratch += [pltpu.VMEM((half, ND, 128), f32), pltpu.VMEM((2, half, ND, 128), f32)]
         scratch += [
             pltpu.SemaphoreType.DMA((max(tiles - 1, 1),)),
             pltpu.SemaphoreType.DMA((max(tiles - 1, 1),)),
             pltpu.SemaphoreType.DMA((3, 14)),
             pltpu.SemaphoreType.DMA((3, 14)),
-            pltpu.SemaphoreType.DMA((6,)),
+            pltpu.SemaphoreType.DMA((8,)),
         ]
         out = jax.ShapeDtypeStruct((nz, nx, ny), f32)
-        vmem = pl.BlockSpec(memory_space=pltpu.VMEM)
+        hbm = pl.BlockSpec(memory_space=pltpu.HBM)
         return pl.pallas_call(
             functools.partial(kernel, (tiles, strips * subs, subs)),
             out_shape=(out, out),
-            in_specs=[pl.BlockSpec(memory_space=pltpu.HBM)] * 6,
-            out_specs=(vmem, vmem),
+            in_specs=[hbm] * 6,
+            out_specs=(hbm, hbm),
             scratch_shapes=scratch,
             compiler_params=pltpu.CompilerParams(
-                collective_id=0, has_side_effects=True, vmem_limit_bytes=40 * 1024 * 1024
+                collective_id=0, has_side_effects=True, vmem_limit_bytes=VMEM_BYTES
             ),
         )(
             right_side, horiz_coef, vert_coef,

time: 39.9 us -> 36 us (0.902)
  local copies, waits for them, and re-layouts: 5.51 us -> 2.74 us
  Pallas kernels: 33.4 us -> 32.5 us
    unnamed x14 -> x4, local copies, waits for them, and re-layouts: 5.51 us -> 2.74 us
    pallas_call x1, Pallas kernels: 33.4 us -> 32.5 us  [body(): pl.pallas_call(functools.partial(kernel, (tiles, strips * subs, subs)), o...]
where the time goes in v2:
time: 36 us; the launch traced here: 35.9 us
  Pallas kernels  32.5 us (90%)
  local copies, waits for them, and re-layouts  2.74 us (8%)
  between operations  0.65 us (2%)
    pallas_call x1, Pallas kernels, body(): pl.pallas_call(functools.partial(kernel, (tiles, strips * subs, subs)), o...  32.5 us
    unnamed x4, local copies, waits for them, and re-layouts  2.74 us

profile of v2, /device:TPU:0, one launch (start us, length us, event | category | flops | bytes accessed | tf_op | source)
XLA Modules:
  0.0 35.9 jit_solution(2390588161431907039)
XLA Ops:
  0.6 32.5 %shard_map.77 = (f32[16,32,256]{2,1,0:T(8,128)}, f32[16,32,256]{2,1,0:T(8,128)}) custom-call(f32[16,32,256]{2,1,0:T(8,128)} %rs.1, f32[32,256]{1,0:T(8,128)} %kh.1, f32[32,256]{1,0:T(8,128)} %kv.1, s32[4,128]{1,0:T(4,128)} %bitcast.3, s32[4,128]{1,0:T(4,128)} %bitcast.4, f32[4,128]{1,0:T(4,128)} %bitcast.5), custom_call_target="tpu_custom_call" | custom-call | tf_op jit(solution)/shard_map/pallas_call | solution.py:395
  33.1 0.0 copy-start
  33.1 1.9 %copy.10 = f32[16,32,256]{2,1,0:T(8,128)} copy(f32[16,32,256]{2,1,0:T(8,128)} %get-tuple-element.4) | data formatting | bytes 1048576
  35.1 0.0 copy-done
  35.1 0.8 %copy.11 = f32[16,32,256]{2,1,0:T(8,128)} copy(f32[16,32,256]{2,1,0:T(8,128)S(1)} %copy-done) | data formatting | bytes 1048576
Async XLA Ops:
  33.1 2.0 %copy-start = (f32[16,32,256]{2,1,0:T(8,128)S(1)}, f32[16,32,256]{2,1,0:T(8,128)}, u32[]{:S(2)}) copy-start(f32[16,32,256]{2,1,0:T(8,128)} %get-tuple-element.5) | copy-start | bytes 1572868
